TPU v7x, 128 devices: a whole 4x4x4 slice. The times are simulated.
128 devices in a mesh: dom: 8 (over z, x_lo), feat: 16 (over y, x_hi, core).
Axes of the slice: x: 4 (x_hi: 2, x_lo: 2; x = x_hi * 2 + x_lo), y: 4, z: 4, core: 2. Of those that a mesh axis runs over, the one named last changes fastest.
Arguments:
- particles: bfloat16 [832, 196608], P('dom', 'feat'), may hold values from -13 to 13
- gradients: bfloat16 [832, 196608], P('dom', 'feat'), may hold values from -6 to 6
- spread: float32 [1], replicated, may hold values from 1 to 2
Outputs:
- drive: float32 [832, 196608], P('dom', 'feat')
- repel: float32 [832, 196608], P('dom', 'feat')
All inputs are finite; a program needn't handle non-finite values.
Results may differ from a plain program's by a relative error of at most 0.0028.
Values may be sent and summed in bfloat16 or wider, within the bound.
A program may use at most 128 MiB of HBM per device.

v0:
```python
import jax
import jax.numpy as jnp
from jax import lax
from jax.sharding import PartitionSpec as P

DIMS = 196608


def passed_along(value, axis, steps):
    count = lax.axis_size(axis)
    pairs = [(source, (source + steps) % count) for source in range(count)]
    return lax.ppermute(value, axis, pairs)


def row_squares(block):
    wide = block.astype(jnp.float32)
    return jnp.sum(wide * wide, axis=1)


def inner_rows(left, right):
    return lax.dot_general(
        left, right, (((1,), (1,)), ((), ())), preferred_element_type=jnp.float32
    )


def per_device(particles, gradients, spread):
    width = DIMS * spread[0]
    local_sq = row_squares(particles)

    def add_tile(carry, other_x, other_g):
        drive_sum, pulled_sum, total_sum = carry
        partial_value = (
            local_sq[:, None] + row_squares(other_x)[None, :] - 2.0 * inner_rows(particles, other_x)
        )
        dist = lax.psum(partial_value, "feat")
        kern = jnp.exp(-dist / width).astype(jnp.bfloat16)
        total_sum = total_sum + jnp.sum(kern.astype(jnp.float32), axis=1)
        drive_sum = drive_sum + jnp.dot(kern, other_g, preferred_element_type=jnp.float32)
        pulled_sum = pulled_sum + jnp.dot(kern, other_x, preferred_element_type=jnp.float32)
        return (drive_sum, pulled_sum, total_sum)

    zeros_big = jnp.zeros(particles.shape, jnp.float32)
    start = add_tile(
        (zeros_big, zeros_big, jnp.zeros((particles.shape[0],), jnp.float32)), particles, gradients
    )

    def advance(index, state):
        carry, held_x, held_g = state
        moved_x, moved_g = passed_along((held_x, held_g), "dom", 1)
        return (add_tile(carry, moved_x, moved_g), moved_x, moved_g)

    final, ignored_x, ignored_g = lax.fori_loop(
        1, lax.axis_size("dom"), advance, (start, particles, gradients)
    )
    drive, pulled, totals = final
    repel = totals[:, None] * particles.astype(jnp.float32) - pulled
    return (drive, repel)


def solution(mesh):
    return jax.shard_map(
        per_device,
        mesh=mesh,
        in_specs=(P("dom", "feat"), P("dom", "feat"), P()),
        out_specs=(P("dom", "feat"), P("dom", "feat")),
        check_vma=False,
    )
```

profile of v0, /device:TPU:1, one launch (start us, length us, event | category | flops | bytes accessed | tf_op | source)
XLA Modules:
  0.0 1373.4 jit_solution(9894783613137121380)
XLA Ops:
  10.3 65.4 %psum.14 = f32[104,104]{1,0:T(8,128)S(1)} all-reduce(f32[104,104]{1,0:T(8,128)S(1)} %fusion.2), channel_id=1, replica_groups=mesh['dom'=8,'feat'=16] {'feat'}, use_global_device_ids=true, to_apply=%region_1.0 | all-reduce | flops 10816 | bytes 86528 | tf_op jit(solution)/shard_map/psum | solution.py:35
  79.3 4.9 fusion.3
  84.1 4.9 fusion.4
  89.0 1278.2 %while.18 = (s32[]{:T(128)}, f32[104,12288]{1,0:T(8,128)}, f32[104,12288]{1,0:T(8,128)}, f32[104]{0:T(128)S(1)}, bf16[104,12288]{1,0:T(8,128)(2,1)}, /*index=5*/...) while((s32[]{:T(128)}, f32[104,12288]{1,0:T(8,128)}, ...), condition=%wide.region_7.8_spmd, body=%wide.region_3.7_spmd.sunk | while | flops 803929088 | bytes 135704128 | solution.py:52
  91.8 51.0 %collective-permute-done = bf16[104,12288]{1,0:T(8,128)(2,1)S(1)} collective-permute-done((bf16[104,12288]{1,0:T(8,128)(2,1)}, bf16[104,12288]{1,0:T(8,128)(2,1)S(1)}, u32[]{:S(2)}, u32[]{:S(2)}) %collective-permute-start) | collective-permute-done | bytes 2555936 | tf_op jit(solution)/shard_map/while/body/eval_jaxpr/ppermute | solution.py:12
  146.0 110.6 %psum.16 = f32[104,104]{1,0:T(8,128)S(1)} all-reduce(f32[104,104]{1,0:T(8,128)S(1)} %add_subtract_fusion.2), channel_id=1, replica_groups=mesh['dom'=8,'feat'=16] {'feat'}, use_global_device_ids=true, to_apply=%region_5.0 | all-reduce | flops 10816 | bytes 86528 | tf_op jit(solution)/shard_map/while/body/eval_jaxpr/psum | solution.py:35
  258.3 4.2 copy.22
  273.5 50.6 %collective-permute-done = bf16[104,12288]{1,0:T(8,128)(2,1)S(1)} collective-permute-done((bf16[104,12288]{1,0:T(8,128)(2,1)}, bf16[104,12288]{1,0:T(8,128)(2,1)S(1)}, u32[]{:S(2)}, u32[]{:S(2)}) %collective-permute-start) | collective-permute-done | bytes 2555936 | tf_op jit(solution)/shard_map/while/body/eval_jaxpr/ppermute | solution.py:12
  327.2 113.3 %psum.16 = f32[104,104]{1,0:T(8,128)S(1)} all-reduce(f32[104,104]{1,0:T(8,128)S(1)} %add_subtract_fusion.2), channel_id=1, replica_groups=mesh['dom'=8,'feat'=16] {'feat'}, use_global_device_ids=true, to_apply=%region_5.0 | all-reduce | flops 10816 | bytes 86528 | tf_op jit(solution)/shard_map/while/body/eval_jaxpr/psum | solution.py:35
  442.2 4.2 copy.22
  457.4 50.6 %collective-permute-done = bf16[104,12288]{1,0:T(8,128)(2,1)S(1)} collective-permute-done((bf16[104,12288]{1,0:T(8,128)(2,1)}, bf16[104,12288]{1,0:T(8,128)(2,1)S(1)}, u32[]{:S(2)}, u32[]{:S(2)}) %collective-permute-start) | collective-permute-done | bytes 2555936 | tf_op jit(solution)/shard_map/while/body/eval_jaxpr/ppermute | solution.py:12
  511.1 111.1 %psum.16 = f32[104,104]{1,0:T(8,128)S(1)} all-reduce(f32[104,104]{1,0:T(8,128)S(1)} %add_subtract_fusion.2), channel_id=1, replica_groups=mesh['dom'=8,'feat'=16] {'feat'}, use_global_device_ids=true, to_apply=%region_5.0 | all-reduce | flops 10816 | bytes 86528 | tf_op jit(solution)/shard_map/while/body/eval_jaxpr/psum | solution.py:35
  623.9 4.2 copy.22
  639.1 50.6 %collective-permute-done = bf16[104,12288]{1,0:T(8,128)(2,1)S(1)} collective-permute-done((bf16[104,12288]{1,0:T(8,128)(2,1)}, bf16[104,12288]{1,0:T(8,128)(2,1)S(1)}, u32[]{:S(2)}, u32[]{:S(2)}) %collective-permute-start) | collective-permute-done | bytes 2555936 | tf_op jit(solution)/shard_map/while/body/eval_jaxpr/ppermute | solution.py:12
  692.8 113.3 %psum.16 = f32[104,104]{1,0:T(8,128)S(1)} all-reduce(f32[104,104]{1,0:T(8,128)S(1)} %add_subtract_fusion.2), channel_id=1, replica_groups=mesh['dom'=8,'feat'=16] {'feat'}, use_global_device_ids=true, to_apply=%region_5.0 | all-reduce | flops 10816 | bytes 86528 | tf_op jit(solution)/shard_map/while/body/eval_jaxpr/psum | solution.py:35
  822.7 50.9 %collective-permute-done = bf16[104,12288]{1,0:T(8,128)(2,1)S(1)} collective-permute-done((bf16[104,12288]{1,0:T(8,128)(2,1)}, bf16[104,12288]{1,0:T(8,128)(2,1)S(1)}, u32[]{:S(2)}, u32[]{:S(2)}) %collective-permute-start) | collective-permute-done | bytes 2555936 | tf_op jit(solution)/shard_map/while/body/eval_jaxpr/ppermute | solution.py:12
  876.7 111.1 %psum.16 = f32[104,104]{1,0:T(8,128)S(1)} all-reduce(f32[104,104]{1,0:T(8,128)S(1)} %add_subtract_fusion.2), channel_id=1, replica_groups=mesh['dom'=8,'feat'=16] {'feat'}, use_global_device_ids=true, to_apply=%region_5.0 | all-reduce | flops 10816 | bytes 86528 | tf_op jit(solution)/shard_map/while/body/eval_jaxpr/psum | solution.py:35
  989.5 4.2 copy.22
  1004.4 50.9 %collective-permute-done = bf16[104,12288]{1,0:T(8,128)(2,1)S(1)} collective-permute-done((bf16[104,12288]{1,0:T(8,128)(2,1)}, bf16[104,12288]{1,0:T(8,128)(2,1)S(1)}, u32[]{:S(2)}, u32[]{:S(2)}) %collective-permute-start) | collective-permute-done | bytes 2555936 | tf_op jit(solution)/shard_map/while/body/eval_jaxpr/ppermute | solution.py:12
  1058.4 113.0 %psum.16 = f32[104,104]{1,0:T(8,128)S(1)} all-reduce(f32[104,104]{1,0:T(8,128)S(1)} %add_subtract_fusion.2), channel_id=1, replica_groups=mesh['dom'=8,'feat'=16] {'feat'}, use_global_device_ids=true, to_apply=%region_5.0 | all-reduce | flops 10816 | bytes 86528 | tf_op jit(solution)/shard_map/while/body/eval_jaxpr/psum | solution.py:35
  1185.8 53.0 %collective-permute-done = bf16[104,12288]{1,0:T(8,128)(2,1)S(1)} collective-permute-done((bf16[104,12288]{1,0:T(8,128)(2,1)}, bf16[104,12288]{1,0:T(8,128)(2,1)S(1)}, u32[]{:S(2)}, u32[]{:S(2)}) %collective-permute-start) | collective-permute-done | bytes 2555936 | tf_op jit(solution)/shard_map/while/body/eval_jaxpr/ppermute | solution.py:12
  1242.0 111.1 %psum.16 = f32[104,104]{1,0:T(8,128)S(1)} all-reduce(f32[104,104]{1,0:T(8,128)S(1)} %add_subtract_fusion.2), channel_id=1, replica_groups=mesh['dom'=8,'feat'=16] {'feat'}, use_global_device_ids=true, to_apply=%region_5.0 | all-reduce | flops 10816 | bytes 86528 | tf_op jit(solution)/shard_map/while/body/eval_jaxpr/psum | solution.py:35
  1354.7 4.2 copy.22
  1367.2 6.2 fusion.1
  (175 shorter events, 128.4 us)
Async XLA Ops:
  89.0 53.8 %collective-permute-start = (bf16[104,12288]{1,0:T(8,128)(2,1)}, bf16[104,12288]{1,0:T(8,128)(2,1)S(1)}, u32[]{:S(2)}, u32[]{:S(2)}) collective-permute-start(bf16[104,12288]{1,0:T(8,128)(2,1)} %get-tuple-element.149), channel_id=1, source_target_pairs={{0,16},{16,32},{32,48},{48,64},{64,80},{80,96},{96,112},{112,0},{1... | collective-permute-start | bytes 7667720 | tf_op jit(solution)/shard_map/while/body/eval_jaxpr/ppermute | solution.py:12
  89.3 169.0 %collective-permute-start.1 = (bf16[104,12288]{1,0:T(8,128)(2,1)}, bf16[104,12288]{1,0:T(8,128)(2,1)}, u32[]{:S(2)}, u32[]{:S(2)}) collective-permute-start(bf16[104,12288]{1,0:T(8,128)(2,1)} %get-tuple-element.150), channel_id=1, source_target_pairs={{0,16},{16,32},{32,48},{48,64},{64,80},{80,96},{96,112},{112,0},{1... | collective-permute-start | bytes 7667720 | tf_op jit(solution)/shard_map/while/body/eval_jaxpr/ppermute | solution.py:12
  256.7 5.7 slice-start.2
  258.3 7.8 slice-start
  270.7 53.4 %collective-permute-start = (bf16[104,12288]{1,0:T(8,128)(2,1)}, bf16[104,12288]{1,0:T(8,128)(2,1)S(1)}, u32[]{:S(2)}, u32[]{:S(2)}) collective-permute-start(bf16[104,12288]{1,0:T(8,128)(2,1)} %get-tuple-element.149), channel_id=1, source_target_pairs={{0,16},{16,32},{32,48},{48,64},{64,80},{80,96},{96,112},{112,0},{1... | collective-permute-start | bytes 7667720 | tf_op jit(solution)/shard_map/while/body/eval_jaxpr/ppermute | solution.py:12
  273.2 169.0 %collective-permute-start.1 = (bf16[104,12288]{1,0:T(8,128)(2,1)}, bf16[104,12288]{1,0:T(8,128)(2,1)}, u32[]{:S(2)}, u32[]{:S(2)}) collective-permute-start(bf16[104,12288]{1,0:T(8,128)(2,1)} %get-tuple-element.150), channel_id=1, source_target_pairs={{0,16},{16,32},{32,48},{48,64},{64,80},{80,96},{96,112},{112,0},{1... | collective-permute-start | bytes 7667720 | tf_op jit(solution)/shard_map/while/body/eval_jaxpr/ppermute | solution.py:12
  440.6 5.7 slice-start.2
  442.2 7.8 slice-start
  454.6 53.4 %collective-permute-start = (bf16[104,12288]{1,0:T(8,128)(2,1)}, bf16[104,12288]{1,0:T(8,128)(2,1)S(1)}, u32[]{:S(2)}, u32[]{:S(2)}) collective-permute-start(bf16[104,12288]{1,0:T(8,128)(2,1)} %get-tuple-element.149), channel_id=1, source_target_pairs={{0,16},{16,32},{32,48},{48,64},{64,80},{80,96},{96,112},{112,0},{1... | collective-permute-start | bytes 7667720 | tf_op jit(solution)/shard_map/while/body/eval_jaxpr/ppermute | solution.py:12
  454.9 169.0 %collective-permute-start.1 = (bf16[104,12288]{1,0:T(8,128)(2,1)}, bf16[104,12288]{1,0:T(8,128)(2,1)}, u32[]{:S(2)}, u32[]{:S(2)}) collective-permute-start(bf16[104,12288]{1,0:T(8,128)(2,1)} %get-tuple-element.150), channel_id=1, source_target_pairs={{0,16},{16,32},{32,48},{48,64},{64,80},{80,96},{96,112},{112,0},{1... | collective-permute-start | bytes 7667720 | tf_op jit(solution)/shard_map/while/body/eval_jaxpr/ppermute | solution.py:12
  623.9 7.8 slice-start
  636.3 53.4 %collective-permute-start = (bf16[104,12288]{1,0:T(8,128)(2,1)}, bf16[104,12288]{1,0:T(8,128)(2,1)S(1)}, u32[]{:S(2)}, u32[]{:S(2)}) collective-permute-start(bf16[104,12288]{1,0:T(8,128)(2,1)} %get-tuple-element.149), channel_id=1, source_target_pairs={{0,16},{16,32},{32,48},{48,64},{64,80},{80,96},{96,112},{112,0},{1... | collective-permute-start | bytes 7667720 | tf_op jit(solution)/shard_map/while/body/eval_jaxpr/ppermute | solution.py:12
  638.8 169.0 %collective-permute-start.1 = (bf16[104,12288]{1,0:T(8,128)(2,1)}, bf16[104,12288]{1,0:T(8,128)(2,1)}, u32[]{:S(2)}, u32[]{:S(2)}) collective-permute-start(bf16[104,12288]{1,0:T(8,128)(2,1)} %get-tuple-element.150), channel_id=1, source_target_pairs={{0,16},{16,32},{32,48},{48,64},{64,80},{80,96},{96,112},{112,0},{1... | collective-permute-start | bytes 7667720 | tf_op jit(solution)/shard_map/while/body/eval_jaxpr/ppermute | solution.py:12
  806.2 5.7 slice-start.2
  807.8 7.8 slice-start
  820.2 53.4 %collective-permute-start = (bf16[104,12288]{1,0:T(8,128)(2,1)}, bf16[104,12288]{1,0:T(8,128)(2,1)S(1)}, u32[]{:S(2)}, u32[]{:S(2)}) collective-permute-start(bf16[104,12288]{1,0:T(8,128)(2,1)} %get-tuple-element.149), channel_id=1, source_target_pairs={{0,16},{16,32},{32,48},{48,64},{64,80},{80,96},{96,112},{112,0},{1... | collective-permute-start | bytes 7667720 | tf_op jit(solution)/shard_map/while/body/eval_jaxpr/ppermute | solution.py:12
  820.5 169.0 %collective-permute-start.1 = (bf16[104,12288]{1,0:T(8,128)(2,1)}, bf16[104,12288]{1,0:T(8,128)(2,1)}, u32[]{:S(2)}, u32[]{:S(2)}) collective-permute-start(bf16[104,12288]{1,0:T(8,128)(2,1)} %get-tuple-element.150), channel_id=1, source_target_pairs={{0,16},{16,32},{32,48},{48,64},{64,80},{80,96},{96,112},{112,0},{1... | collective-permute-start | bytes 7667720 | tf_op jit(solution)/shard_map/while/body/eval_jaxpr/ppermute | solution.py:12
  989.4 7.8 slice-start
  1001.9 53.4 %collective-permute-start = (bf16[104,12288]{1,0:T(8,128)(2,1)}, bf16[104,12288]{1,0:T(8,128)(2,1)S(1)}, u32[]{:S(2)}, u32[]{:S(2)}) collective-permute-start(bf16[104,12288]{1,0:T(8,128)(2,1)} %get-tuple-element.149), channel_id=1, source_target_pairs={{0,16},{16,32},{32,48},{48,64},{64,80},{80,96},{96,112},{112,0},{1... | collective-permute-start | bytes 7667720 | tf_op jit(solution)/shard_map/while/body/eval_jaxpr/ppermute | solution.py:12
  1004.1 169.0 %collective-permute-start.1 = (bf16[104,12288]{1,0:T(8,128)(2,1)}, bf16[104,12288]{1,0:T(8,128)(2,1)}, u32[]{:S(2)}, u32[]{:S(2)}) collective-permute-start(bf16[104,12288]{1,0:T(8,128)(2,1)} %get-tuple-element.150), channel_id=1, source_target_pairs={{0,16},{16,32},{32,48},{48,64},{64,80},{80,96},{96,112},{112,0},{1... | collective-permute-start | bytes 7667720 | tf_op jit(solution)/shard_map/while/body/eval_jaxpr/ppermute | solution.py:12
  1173.0 7.8 slice-start
  1185.5 53.4 %collective-permute-start = (bf16[104,12288]{1,0:T(8,128)(2,1)}, bf16[104,12288]{1,0:T(8,128)(2,1)S(1)}, u32[]{:S(2)}, u32[]{:S(2)}) collective-permute-start(bf16[104,12288]{1,0:T(8,128)(2,1)} %get-tuple-element.149), channel_id=1, source_target_pairs={{0,16},{16,32},{32,48},{48,64},{64,80},{80,96},{96,112},{112,0},{1... | collective-permute-start | bytes 7667720 | tf_op jit(solution)/shard_map/while/body/eval_jaxpr/ppermute | solution.py:12
  1185.8 169.0 %collective-permute-start.1 = (bf16[104,12288]{1,0:T(8,128)(2,1)}, bf16[104,12288]{1,0:T(8,128)(2,1)}, u32[]{:S(2)}, u32[]{:S(2)}) collective-permute-start(bf16[104,12288]{1,0:T(8,128)(2,1)} %get-tuple-element.150), channel_id=1, source_target_pairs={{0,16},{16,32},{32,48},{48,64},{64,80},{80,96},{96,112},{112,0},{1... | collective-permute-start | bytes 7667720 | tf_op jit(solution)/shard_map/while/body/eval_jaxpr/ppermute | solution.py:12
  1354.7 7.8 slice-start
  (32 other events, 120.7 us)
where the time goes:
time: 1380 us; the launch traced here: 1370 us
  blocking collectives  849 us (62%)
  waiting for transfers between devices  357 us (26%)
  matrix products  68.5 us (5%)
  local copies, waits for them, and re-layouts  66.5 us (5%)
  starting transfers between devices  16.7 us (1%)
    psum x8, blocking collectives, add_tile(): dist = lax.psum(partial_value, 'feat')  849 us
    ppermute x14, waiting for transfers between devices, passed_along(): return lax.ppermute(value, axis, pairs)  357 us
    while x98, local copies, waits for them, and re-layouts  59.7 us
    dot_general x8, matrix products, add_tile(): jnp.dot(kern, other_g, preferred_element_type=jnp.float32)  29.9 us
  transfers between devices with their start and end apart: 14, of which 7 were waited for; matrix products, arithmetic and copies ran while one was open for 2% of the time, Pallas kernels for 0%

commit v1 on v0

v1 whole, which is shorter than its diff:
```python
import jax
import jax.numpy as jnp
from jax import lax
from jax.experimental import pallas as pl
from jax.experimental.pallas import tpu as pltpu
from jax.sharding import PartitionSpec as P

DIMS = 196608
ROWS = 104
COLS = 12288
BLOCKS = 8
WIDTH = COLS // BLOCKS
PAIR = 2 * ROWS
FLAT = 4096
HALF, QUARTER, CHUNK = FLAT // 2, FLAT // 8, FLAT // 128
MESH = pl.DeviceIdType.MESH


def row_of_block(k, i):
    return pl.multiple_of((BLOCKS * k + i) * ROWS, 8)


def kernel(
    x, g, spread, drive_out, repel_out,
    xt, gt, own_gram, sq_col, sq_row, part, from_core, half_sum, half_wire, from_y, quarter_sum, from_zx,
    kern, kern_wide, kern_rows, drive_stage, repel_stage,
    x_send, x_recv, g_send, g_recv, d_send, d_recv, r_send, r_recv, own_sem,
    c_send, c_recv, y_send, y_recv, p_send, p_recv, ap_send, ap_recv, ay_send, ay_recv, ac_send, ac_recv,
):
    dom, feat = lax.axis_index("dom"), lax.axis_index("feat")
    z, x_lo = dom // 2, dom % 2
    y, x_hi, core = feat // 4, (feat // 2) % 2, feat % 2
    xx = x_hi * 2 + x_lo

    def dom_peer(r):
        return (z + r // 2) % 4 * 2 + (x_lo + r % 2) % 2

    def plane_peer(r):
        z2, x2 = (z + r // 4) % 4, (xx + r % 4) % 4
        return z2 * 4 + x2, (z2 * 2 + x2 % 2, y * 4 + x2 // 2 * 2 + core)

    def y_peer(r):
        y2 = (y + r) % 4
        return y2, (dom, y2 * 4 + x_hi * 2 + core)

    sibling = (dom, y * 4 + x_hi * 2 + 1 - core)

    barrier = pltpu.get_barrier_semaphore()

    @pl.loop(1, 16)
    def _(r):
        pl.semaphore_signal(barrier, inc=1, device_id=plane_peer(r)[1], device_id_type=MESH)

    @pl.loop(1, 4)
    def _(r):
        pl.semaphore_signal(barrier, inc=1, device_id=y_peer(r)[1], device_id_type=MESH)

    pl.semaphore_signal(barrier, inc=1, device_id=sibling, device_id_type=MESH)
    pl.semaphore_wait(barrier, 19)

    def columns(block):
        return pl.ds(pl.multiple_of(block * WIDTH, 128), WIDTH)

    def inward(src, dst, send, recv, r):
        to = dom_peer(r)
        return pltpu.make_async_remote_copy(
            src_ref=src.at[:, columns(to)], dst_ref=dst.at[dom], send_sem=send.at[r], recv_sem=recv.at[r],
            device_id=(to, feat), device_id_type=MESH)

    def outward(src, dst, send, recv, r):
        to = dom_peer(r)
        return pltpu.make_async_remote_copy(
            src_ref=src.at[to], dst_ref=dst.at[:, columns(dom)], send_sem=send.at[r], recv_sem=recv.at[r],
            device_id=(to, feat), device_id_type=MESH)

    own_x = pltpu.make_async_copy(x.at[:, columns(dom)], xt.at[dom], own_sem.at[0])
    own_g = pltpu.make_async_copy(g.at[:, columns(dom)], gt.at[dom], own_sem.at[1])

    @pl.loop(1, BLOCKS)
    def _(r):
        inward(x, xt, x_send, x_recv, r).start()

    own_x.start()
    own_g.start()
    part[...] = jnp.zeros_like(part)

    @pl.loop(1, BLOCKS)
    def _(r):
        inward(x, xt, x_send, x_recv, r).wait_send()
        inward(g, gt, g_send, g_recv, r).start()

    own_x.wait()

    @pl.loop(1, BLOCKS)
    def _(r):
        inward(x, xt, x_send, x_recv, r).wait_recv()

    def gram(i, j):
        return lax.dot_general(xt[i], xt[j], (((1,), (1,)), ((), ())), preferred_element_type=jnp.float32)

    on_diagonal = lax.broadcasted_iota(jnp.int32, (ROWS, ROWS), 0) == lax.broadcasted_iota(jnp.int32, (ROWS, ROWS), 1)

    @pl.loop(0, BLOCKS)
    def _(i):
        block = gram(i, i)
        own_gram[i] = block
        picked = jnp.where(on_diagonal, block, 0.0)
        sq_col[i] = jnp.sum(picked, axis=1, keepdims=True)
        sq_row[i] = jnp.sum(picked, axis=0, keepdims=True)

    def partial_dist(k, i):
        j = (i + k) % BLOCKS
        inner = own_gram[i] if k == 0 else gram(i, j)
        return sq_col[i] + sq_row[j] - 2.0 * inner

    def store_pair(k, q):
        both = jnp.concatenate([partial_dist(k, 2 * q), partial_dist(k, 2 * q + 1)], axis=0)
        part[pl.ds(pl.multiple_of((4 * k + q) * PAIR, 16), PAIR), 0:ROWS] = both.astype(jnp.bfloat16)

    @pl.loop(0, 4)
    def _(q):
        for k in range(4):
            store_pair(k, q)

    @pl.loop(0, 2)
    def _(q):
        store_pair(4, q)

    def half_rows(which):
        return pl.ds(pl.multiple_of(which * HALF, 16), HALF)

    to_core = pltpu.make_async_remote_copy(
        src_ref=part.at[half_rows(1 - core)], dst_ref=from_core, send_sem=c_send, recv_sem=c_recv,
        device_id=sibling, device_id_type=MESH)
    to_core.start()
    to_core.wait()
    half_sum[...] = part[half_rows(core)].astype(jnp.float32) + from_core[...].astype(jnp.float32)
    half_wire[...] = half_sum[...].astype(jnp.bfloat16)

    def to_y(r):
        y2, device = y_peer(r)
        return pltpu.make_async_remote_copy(
            src_ref=half_wire.at[pl.ds(pl.multiple_of(y2 * QUARTER, 16), QUARTER)], dst_ref=from_y.at[r],
            send_sem=y_send.at[r], recv_sem=y_recv.at[r], device_id=device, device_id_type=MESH)

    for r in range(1, 4):
        to_y(r).start()
    total = half_sum[pl.ds(pl.multiple_of(y * QUARTER, 16), QUARTER)]
    for r in range(1, 4):
        to_y(r).wait()
    for r in range(1, 4):
        total = total + from_y[r].astype(jnp.float32)
    quarter_sum[...] = total

    member = z * 4 + xx

    def to_plane(r):
        m2, device = plane_peer(r)
        return pltpu.make_async_remote_copy(
            src_ref=quarter_sum.at[pl.ds(pl.multiple_of(m2 * CHUNK, 8), CHUNK)], dst_ref=from_zx.at[r],
            send_sem=p_send.at[r], recv_sem=p_recv.at[r], device_id=device, device_id_type=MESH)

    @pl.loop(1, 16)
    def _(r):
        to_plane(r).start()

    from_zx[0] = quarter_sum[pl.ds(pl.multiple_of(member * CHUNK, 8), CHUNK)]

    @pl.loop(1, 16)
    def _(r):
        to_plane(r).wait()

    dist = jnp.sum(from_zx[...], axis=0)
    width = DIMS * spread[0]
    base = pl.multiple_of(core * HALF + y * QUARTER, 16)
    mine = pl.ds(pl.multiple_of(base + member * CHUNK, 16), CHUNK)
    kern[mine] = jnp.exp(-dist / width).astype(jnp.bfloat16)

    def kern_to_plane(r):
        return pltpu.make_async_remote_copy(
            src_ref=kern.at[mine], dst_ref=kern.at[mine], send_sem=ap_send.at[r], recv_sem=ap_recv.at[r],
            device_id=plane_peer(r)[1], device_id_type=MESH)

    @pl.loop(1, 16)
    def _(r):
        kern_to_plane(r).start()

    @pl.loop(1, 16)
    def _(r):
        kern_to_plane(r).wait()

    quarter = pl.ds(base, QUARTER)

    def kern_to_y(r):
        return pltpu.make_async_remote_copy(
            src_ref=kern.at[quarter], dst_ref=kern.at[quarter], send_sem=ay_send.at[r], recv_sem=ay_recv.at[r],
            device_id=y_peer(r)[1], device_id_type=MESH)

    def kern_to_core(r):
        y2 = (y + 4 - r) % 4
        rows = pl.ds(pl.multiple_of(core * HALF + y2 * QUARTER, 16), QUARTER)
        return pltpu.make_async_remote_copy(
            src_ref=kern.at[rows], dst_ref=kern.at[rows], send_sem=ac_send.at[r], recv_sem=ac_recv.at[r],
            device_id=sibling, device_id_type=MESH)

    for r in range(1, 4):
        kern_to_y(r).start()
    kern_to_core(0).start()
    for r in range(1, 4):
        kern_to_y(r).wait_recv()
        kern_to_core(r).start()
    for r in range(4):
        kern_to_core(r).wait()
    for r in range(1, 4):
        kern_to_y(r).wait_send()
    kern_wide[...] = kern[...].astype(jnp.float32)

    def block(k, i):
        return kern_wide[pl.ds(row_of_block(k, i), ROWS), 0:ROWS]

    def kern_block(i, k):
        j = (i + k) % BLOCKS
        if k < 4:
            return block(k, i)
        if k > 4:
            return block(BLOCKS - k, j).T
        across = block(4, i % 4)
        return jnp.where(i < 4, across, across.T)

    @pl.loop(1, BLOCKS + 1)
    def _(step):
        r = step % BLOCKS
        i = dom_peer(r)
        totals = jnp.zeros((ROWS, 1), jnp.float32)
        pulled = jnp.zeros((ROWS, WIDTH), jnp.float32)
        for k in range(BLOCKS):
            wide = kern_block(i, k)
            totals = totals + jnp.sum(wide, axis=1, keepdims=True)
            narrow = wide.astype(jnp.bfloat16)
            kern_rows[i, k] = narrow
            pulled = pulled + jnp.dot(narrow, xt[(i + k) % BLOCKS], preferred_element_type=jnp.float32)
        repel_stage[i] = (totals * xt[i].astype(jnp.float32) - pulled).astype(jnp.bfloat16)

        @pl.when(step < BLOCKS)
        def _():
            outward(repel_stage, repel_out, r_send, r_recv, r).start()

    own_g.wait()

    @pl.loop(1, BLOCKS)
    def _(r):
        inward(g, gt, g_send, g_recv, r).wait()

    @pl.loop(1, BLOCKS + 1)
    def _(step):
        r = step % BLOCKS
        i = dom_peer(r)
        driven = jnp.zeros((ROWS, WIDTH), jnp.float32)
        for k in range(BLOCKS):
            driven = driven + jnp.dot(kern_rows[i, k], gt[(i + k) % BLOCKS], preferred_element_type=jnp.float32)
        drive_stage[i] = driven.astype(jnp.bfloat16)

        @pl.when(step < BLOCKS)
        def _():
            outward(drive_stage, drive_out, d_send, d_recv, r).start()

    own_r = pltpu.make_async_copy(repel_stage.at[dom], repel_out.at[:, columns(dom)], own_sem.at[0])
    own_d = pltpu.make_async_copy(drive_stage.at[dom], drive_out.at[:, columns(dom)], own_sem.at[1])
    own_r.start()
    own_d.start()
    own_r.wait()
    own_d.wait()

    @pl.loop(1, BLOCKS)
    def _(r):
        outward(repel_stage, repel_out, r_send, r_recv, r).wait()

    @pl.loop(1, BLOCKS)
    def _(r):
        outward(drive_stage, drive_out, d_send, d_recv, r).wait()


def per_device(particles, gradients, spread):
    bf16, f32 = jnp.bfloat16, jnp.float32
    vmem, dma = pltpu.VMEM, pltpu.SemaphoreType.DMA
    slab = (BLOCKS, ROWS, WIDTH)
    drive, repel = pl.pallas_call(
        kernel,
        out_shape=[jax.ShapeDtypeStruct((ROWS, COLS), bf16)] * 2,
        in_specs=[pl.BlockSpec(memory_space=pl.ANY)] * 2 + [pl.BlockSpec(memory_space=pltpu.SMEM)],
        out_specs=[pl.BlockSpec(memory_space=pl.ANY)] * 2,
        scratch_shapes=[
            vmem(slab, bf16), vmem(slab, bf16),
            vmem((BLOCKS, ROWS, ROWS), f32), vmem((BLOCKS, ROWS, 1), f32), vmem((BLOCKS, 1, ROWS), f32),
            vmem((FLAT, 128), bf16), vmem((HALF, 128), bf16), vmem((HALF, 128), f32), vmem((HALF, 128), bf16),
            vmem((4, QUARTER, 128), bf16), vmem((QUARTER, 128), f32), vmem((16, CHUNK, 128), f32),
            vmem((FLAT, 128), bf16), vmem((FLAT, 128), f32), vmem((BLOCKS, BLOCKS, ROWS, ROWS), bf16),
            vmem(slab, bf16), vmem(slab, bf16),
        ]
        + [dma((BLOCKS,))] * 8 + [dma((2,))]
        + [dma(()), dma(()), dma((4,)), dma((4,)), dma((16,)), dma((16,))]
        + [dma((16,)), dma((16,)), dma((4,)), dma((4,)), dma((4,)), dma((4,))],
        compiler_params=pltpu.CompilerParams(
            collective_id=0, has_side_effects=True, vmem_limit_bytes=56 * 2**20),
        name="svgd",
    )(particles, gradients, spread)
    return drive.astype(f32), repel.astype(f32)


def solution(mesh):
    return jax.shard_map(
        per_device,
        mesh=mesh,
        in_specs=(P("dom", "feat"), P("dom", "feat"), P()),
        out_specs=(P("dom", "feat"), P("dom", "feat")),
        check_vma=False,
    )
```

time: 1380 us -> 155 us (0.11)
  blocking collectives: 849 us -> 0 us
  waiting for transfers between devices: 357 us -> 0 us
  Pallas kernels: 0 us -> 146 us
  matrix products: 68.5 us -> 0 us
  local copies, waits for them, and re-layouts: 66.5 us -> 0.01 us
  starting transfers between devices: 16.7 us -> 0 us
    psum x8 -> x0, blocking collectives: 849 us -> none  [add_tile(): dist = lax.psum(partial_value, 'feat')]
    ppermute x14 -> x0, waiting for transfers between devices: 357 us -> none  [passed_along(): return lax.ppermute(value, axis, pairs)]
    pallas_call x0 -> x1, Pallas kernels: none -> 146 us  [per_device(): pl.pallas_call(kernel, out_shape=[jax.ShapeDtypeStruct((ROWS, COLS), bf16...]
    dot_general x24 -> x0, matrix products: 68.5 us -> none  [the longest x8 29.9 us: add_tile(): jnp.dot(kern, other_g, preferred_element_type=jnp.float32)]
    while x98 -> x0, local copies, waits for them, and re-layouts: 59.7 us -> none
    ppermute x14 -> x0, starting transfers between devices: 16.7 us -> none  [passed_along(): return lax.ppermute(value, axis, pairs)]
  transfers between devices with their start and end apart: 14 -> 0, of which waited for: 7 -> 0; matrix products, arithmetic and copies ran while one was open for 2% -> 0% of each run, Pallas kernels for 0% -> 0%
where the time goes in v1:
time: 155 us
  Pallas kernels  146 us (94%)
  other arithmetic  7.48 us (5%)
    pallas_call x1, Pallas kernels, per_device(): pl.pallas_call(kernel, out_shape=[jax.ShapeDtypeStruct((ROWS, COLS), bf16...  146 us
    convert_element_type x2, other arithmetic, per_device(): return (drive.astype(f32), repel.astype(f32))  7.48 us

profile of v1, /device:TPU:1, one launch (start us, length us, event | category | flops | bytes accessed | tf_op | source)
XLA Modules:
  0.0 155.1 jit_solution(3018204954529697492)
XLA Ops:
  1.3 146.3 %svgd.1 = (bf16[104,12288]{1,0:T(8,128)(2,1)}, bf16[104,12288]{1,0:T(8,128)(2,1)}) custom-call(bf16[104,12288]{1,0:T(8,128)(2,1)} %x.1, bf16[104,12288]{1,0:T(8,128)(2,1)} %g.1, f32[1]{0:T(128)S(6)} %copy.5.spread), custom_call_target="tpu_custom_call" | custom-call | tf_op jit(solution)/shard_map/svgd/pallas_call | solution.py:287
  147.6 0.0 copy-start
  147.6 4.7 %convert_element_type.6 = f32[104,12288]{1,0:T(8,128)} convert(bf16[104,12288]{1,0:T(8,128)(2,1)} %get-tuple-element.4) | non-fusion elementwise | flops 1277952 | bytes 7667712 | tf_op jit(solution)/shard_map/convert_element_type | solution.py:307
  152.3 0.0 copy-done
  152.3 2.8 %convert_element_type.7 = f32[104,12288]{1,0:T(8,128)} convert(bf16[104,12288]{1,0:T(8,128)(2,1)S(1)} %copy-done) | non-fusion elementwise | flops 1277952 | bytes 7667712 | tf_op jit(solution)/shard_map/convert_element_type | solution.py:307
Async XLA Ops:
  147.6 4.7 %copy-start = (bf16[104,12288]{1,0:T(8,128)(2,1)S(1)}, bf16[104,12288]{1,0:T(8,128)(2,1)}, u32[]{:S(2)}) copy-start(bf16[104,12288]{1,0:T(8,128)(2,1)} %get-tuple-element.5) | copy-start | bytes 7667716

commit v2 on v0

v2 whole, which is shorter than its diff:
```python
import jax
import jax.numpy as jnp
from jax import lax
from jax.experimental import pallas as pl
from jax.experimental.pallas import tpu as pltpu
from jax.sharding import PartitionSpec as P

DIMS = 196608
ROWS = 104
PAD_K, PAD_M = 128, 112
COLS = 12288
BLOCKS = 8
PIECES = 3
WIDTH = COLS // BLOCKS
PIECE = WIDTH // PIECES
G_PIECES = 6
G_PIECE = WIDTH // G_PIECES
G_AT = (1, 0, 1, 1, 1, 2)
PARTS = 2
FLAT = 4096
PART = FLAT // PARTS
HALF, QUARTER, CHUNK = PART // 2, PART // 8, PART // 128
SUPER = [(i, i) for i in range(4)] + [(i, j) for i in range(4) for j in range(i + 1, 4)]
PAIRS = []
for n, (si, sj) in enumerate(SUPER):
    for a in range(2):
        for b in range(2):
            if 2 * si + a <= 2 * sj + b:
                PAIRS.append((2 * si + a, 2 * sj + b, n, a * PAD_K, b * PAD_K))
FIRST = [n for n in range(len(PAIRS)) if (n + 1) * ROWS <= PART]
MESH = pl.DeviceIdType.MESH


def kernel(
    x, g, spread, drive_out, repel_out,
    xt, gt, xd, gd, acc, part, part_wire, from_core, core_sum, core_wire, from_y, y_sum, from_zx,
    kern, kern_wide, full, totals, product, drive_stage, repel_stage, drive_land, repel_land,
    x_send, x_recv, g_send, g_recv, d_send, d_recv, r_send, r_recv, own_sem,
    c_send, c_recv, y_send, y_recv, p_send, p_recv, ap_send, ap_recv, ay_send, ay_recv, ac_send, ac_recv,
):
    f32, bf16 = jnp.float32, jnp.bfloat16
    dom, feat = lax.axis_index("dom"), lax.axis_index("feat")
    z, x_lo = dom // 2, dom % 2
    y, x_hi, core = feat // 4, (feat // 2) % 2, feat % 2
    xx = x_hi * 2 + x_lo
    member = z * 4 + xx

    def dom_peer(r):
        return (z + r // 2) % 4 * 2 + (x_lo + r % 2) % 2

    def plane_peer(r):
        z2, x2 = (z + r // 4) % 4, (xx + r % 4) % 4
        return z2 * 4 + x2, (z2 * 2 + x2 % 2, y * 4 + x2 // 2 * 2 + core)

    def y_peer(r):
        y2 = (y + r) % 4
        return y2, (dom, y2 * 4 + x_hi * 2 + core)

    sibling = (dom, y * 4 + x_hi * 2 + 1 - core)

    barrier = pltpu.get_barrier_semaphore()

    @pl.loop(1, 16)
    def _(r):
        pl.semaphore_signal(barrier, inc=1, device_id=plane_peer(r)[1], device_id_type=MESH)

    @pl.loop(1, 4)
    def _(r):
        pl.semaphore_signal(barrier, inc=1, device_id=y_peer(r)[1], device_id_type=MESH)

    pl.semaphore_signal(barrier, inc=1, device_id=sibling, device_id_type=MESH)
    pl.semaphore_wait(barrier, 19)

    def columns(block, c):
        return pl.ds(pl.multiple_of(block * WIDTH + c * PIECE, 128), PIECE)

    def remote(src, dst, send, recv, device):
        return pltpu.make_async_remote_copy(
            src_ref=src, dst_ref=dst, send_sem=send, recv_sem=recv, device_id=device, device_id_type=MESH)

    def inward(src, dst, send, recv, c, r):
        to = dom_peer(r)
        return remote(src.at[:, columns(to, c)], dst.at[c, dom], send.at[c, r], recv.at[c, r], (to, feat))

    def x_in(c, r):
        return inward(x, xt, x_send, x_recv, c, r)

    def g_in(p, r):
        to, lane = dom_peer(r), p % 2 * G_PIECE
        source = g.at[:, pl.ds(pl.multiple_of(to * WIDTH + p * G_PIECE, 128), G_PIECE)]
        target = gt.at[p // 2, dom, :, pl.ds(lane, G_PIECE)]
        return remote(source, target, g_send.at[p, r], g_recv.at[p, r], (to, feat))

    def start_g(point):
        for p in range(sum(G_AT[:point]), sum(G_AT[: point + 1])):
            @pl.loop(1, BLOCKS)
            def _(r):
                g_in(p, r).start()

    def own_copy(src, dst, which, c):
        return pltpu.make_async_copy(src.at[:, columns(dom, c)], dst.at[c, dom], own_sem.at[which, c])

    for c in range(2):
        @pl.loop(1, BLOCKS)
        def _(r):
            x_in(c, r).start()

    for c in range(PIECES):
        own_copy(x, xt, 0, c).start()
    for c in range(PIECES):
        own_copy(g, gt, 1, c).start()
    part[...] = jnp.zeros_like(part)
    acc[...] = jnp.zeros_like(acc)
    xd[...] = jnp.zeros_like(xd)
    gd[...] = jnp.zeros_like(gd)
    full[...] = jnp.zeros_like(full)

    def spread_out(src, dst, c):
        for b in range(BLOCKS):
            dst[c, b * PAD_K : b * PAD_K + ROWS] = src[c, b]

    for c in range(PIECES):
        @pl.loop(1, BLOCKS)
        def _(r):
            x_in(c, r).wait_send()
            if c == 0:
                x_in(2, r).start()

        if c > 0:
            start_g(c - 1)
        own_copy(x, xt, 0, c).wait()

        @pl.loop(1, BLOCKS)
        def _(r):
            x_in(c, r).wait_recv()

        spread_out(xt, xd, c)
        for n, (si, sj) in enumerate(SUPER):
            left = xd[c, si * 2 * PAD_K : (si + 1) * 2 * PAD_K]
            right = xd[c, sj * 2 * PAD_K : (sj + 1) * 2 * PAD_K]
            acc[n] += lax.dot_general(left, right, (((1,), (1,)), ((), ())), preferred_element_type=f32)

    size = (2 * PAD_K, 2 * PAD_K)
    on_diagonal = lax.broadcasted_iota(jnp.int32, size, 0) == lax.broadcasted_iota(jnp.int32, size, 1)
    sq_col, sq_row = [], []
    for n in range(4):
        picked = jnp.where(on_diagonal, acc[n], 0.0)
        col, row = jnp.sum(picked, axis=1, keepdims=True), jnp.sum(picked, axis=0, keepdims=True)
        for a in (0, PAD_K):
            sq_col.append(col[a : a + ROWS])
            sq_row.append(row[:, a : a + PAD_K])

    def to_core(h):
        rows = pl.ds(pl.multiple_of(h * PART + (1 - core) * HALF, 16), HALF)
        return remote(part_wire.at[rows], from_core.at[h], c_send.at[h], c_recv.at[h], sibling)

    for h in range(PARTS):
        for n, (a, b, s, row, lane) in enumerate(PAIRS):
            if (n in FIRST) == (h == 0) or (h == 0 and n == len(FIRST)):
                inner = acc[s, row : row + ROWS, lane : lane + PAD_K]
                part[n * ROWS : (n + 1) * ROWS] = sq_col[a] + sq_row[b] - 2.0 * inner
        rows = slice(h * PART, (h + 1) * PART)
        part_wire[rows] = part[rows].astype(bf16)
        to_core(h).start()
    start_g(2)

    def to_y(h, r):
        y2, device = y_peer(r)
        rows = pl.ds(pl.multiple_of(y2 * QUARTER, 16), QUARTER)
        return remote(core_wire.at[h, rows], from_y.at[h, r], y_send.at[h, r], y_recv.at[h, r], device)

    def to_plane(h, r):
        m2, device = plane_peer(r)
        rows = pl.ds(pl.multiple_of(m2 * CHUNK, 8), CHUNK)
        return remote(y_sum.at[h, rows], from_zx.at[h, r], p_send.at[h, r], p_recv.at[h, r], device)

    def mine(h):
        return pl.ds(pl.multiple_of(h * PART + core * HALF + y * QUARTER + member * CHUNK, 16), CHUNK)

    def kern_to_plane(h, r):
        rows = kern.at[mine(h)]
        return remote(rows, rows, ap_send.at[h, r], ap_recv.at[h, r], plane_peer(r)[1])

    def kern_to_y(h, r):
        rows = kern.at[pl.ds(pl.multiple_of(h * PART + core * HALF + y * QUARTER, 16), QUARTER)]
        return remote(rows, rows, ay_send.at[h, r], ay_recv.at[h, r], y_peer(r)[1])

    def kern_to_core(h, r):
        y2 = (y + 4 - r) % 4
        rows = kern.at[pl.ds(pl.multiple_of(h * PART + core * HALF + y2 * QUARTER, 16), QUARTER)]
        return remote(rows, rows, ac_send.at[h, r], ac_recv.at[h, r], sibling)

    for h in range(PARTS):
        to_core(h).wait_recv()
        rows = pl.ds(pl.multiple_of(h * PART + core * HALF, 16), HALF)
        core_sum[h] = part[rows] + from_core[h].astype(f32)
        core_wire[h] = core_sum[h].astype(bf16)
        for r in range(1, 4):
            to_y(h, r).start()
    for h in range(PARTS):
        for r in range(1, 4):
            to_y(h, r).wait_recv()
        total = core_sum[h, pl.ds(pl.multiple_of(y * QUARTER, 16), QUARTER)]
        for r in range(1, 4):
            total = total + from_y[h, r].astype(f32)
        y_sum[h] = total

        @pl.loop(1, 16)
        def _(r):
            to_plane(h, r).start()

    start_g(3)
    width = DIMS * spread[0]
    for h in range(PARTS):
        from_zx[h, 0] = y_sum[h, pl.ds(pl.multiple_of(member * CHUNK, 8), CHUNK)]

        @pl.loop(1, 16)
        def _(r):
            to_plane(h, r).wait_recv()

        kern[mine(h)] = jnp.exp(-jnp.sum(from_zx[h], axis=0) / width).astype(bf16)

        @pl.loop(1, 16)
        def _(r):
            kern_to_plane(h, r).start()

    start_g(4)

    for h in range(PARTS):
        @pl.loop(1, 16)
        def _(r):
            kern_to_plane(h, r).wait_recv()

        for r in range(1, 4):
            kern_to_y(h, r).start()
        kern_to_core(h, 0).start()
    start_g(5)
    for h in range(PARTS):
        for r in range(1, 4):
            kern_to_y(h, r).wait_recv()
            kern_to_core(h, r).start()

    real = lax.broadcasted_iota(jnp.int32, (PAD_K, PAD_K), 1) < ROWS
    for h in range(PARTS):
        for r in range(4):
            kern_to_core(h, r).wait_recv()
        rows = slice(h * PART, (h + 1) * PART)
        kern_wide[rows] = kern[rows].astype(f32)
        for n, (a, b, s, row, lane) in enumerate(PAIRS):
            if (n in FIRST) == (h == 0):
                block = kern_wide[n * ROWS : n * ROWS + PAD_K]
                square = jnp.where(real, block, 0.0)
                full[a * PAD_M : a * PAD_M + ROWS, b * PAD_K : (b + 1) * PAD_K] = square[:ROWS].astype(bf16)
                if a != b:
                    across = jnp.where(real, block.T, 0.0)
                    full[b * PAD_M : b * PAD_M + ROWS, a * PAD_K : (a + 1) * PAD_K] = across[:ROWS].astype(bf16)

    @pl.loop(0, BLOCKS)
    def _(i):
        rows = pl.ds(pl.multiple_of(i * PAD_M, 16), ROWS)
        sums = jnp.zeros((ROWS, PAD_K), f32)
        for k in range(BLOCKS):
            sums = sums + full[rows, k * PAD_K : (k + 1) * PAD_K].astype(f32)
        totals[i] = jnp.sum(sums, axis=1, keepdims=True)

    def outward(src, dst, send, recv, c, r):
        to = dom_peer(r)
        return remote(src.at[c, to], dst.at[c, dom], send.at[c, r], recv.at[c, r], (to, feat))

    def r_out(c, r):
        return outward(repel_stage, repel_land, r_send, r_recv, c, r)

    def d_out(c, r):
        return outward(drive_stage, drive_land, d_send, d_recv, c, r)

    def product_rows(i):
        return product[pl.ds(pl.multiple_of(i * PAD_M, 8), ROWS)]

    def repel_rows(c, i):
        here = xd[c, pl.ds(pl.multiple_of(i * PAD_K, 16), ROWS)].astype(f32)
        return totals[i] * here - product_rows(i)

    @pl.loop(0, PIECES)
    def _(c):
        product[...] = jnp.dot(full[...], xd[c], preferred_element_type=f32)

        @pl.loop(1, BLOCKS)
        def _(r):
            i = dom_peer(r)
            repel_stage[c, i] = repel_rows(c, i).astype(bf16)
            r_out(c, r).start()

        repel_out[:, columns(dom, c)] = repel_rows(c, dom)

    for c in range(PIECES):
        own_copy(g, gt, 1, c).wait()

        for p in (2 * c, 2 * c + 1):
            @pl.loop(1, BLOCKS)
            def _(r):
                g_in(p, r).wait()

        spread_out(gt, gd, c)

    @pl.loop(0, PIECES)
    def _(c):
        product[...] = jnp.dot(full[...], gd[c], preferred_element_type=f32)

        @pl.loop(1, BLOCKS)
        def _(r):
            i = dom_peer(r)
            drive_stage[c, i] = product_rows(i).astype(bf16)
            d_out(c, r).start()

        drive_out[:, columns(dom, c)] = product_rows(dom)

    for h in range(PARTS):
        to_core(h).wait_send()
        for r in range(1, 4):
            to_y(h, r).wait_send()
            kern_to_y(h, r).wait_send()
        for r in range(4):
            kern_to_core(h, r).wait_send()

        @pl.loop(1, 16)
        def _(r):
            to_plane(h, r).wait_send()
            kern_to_plane(h, r).wait_send()

    def widen(copy, land, out):
        @pl.loop(0, PIECES)
        def _(c):
            @pl.loop(1, BLOCKS)
            def _(r):
                copy(c, r).wait()
                source = (z + 4 - r // 2) % 4 * 2 + (x_lo + r % 2) % 2
                out[:, columns(source, c)] = land[c, source].astype(f32)

    widen(r_out, repel_land, repel_out)
    widen(d_out, drive_land, drive_out)


def per_device(particles, gradients, spread):
    bf16, f32 = jnp.bfloat16, jnp.float32
    vmem, dma = pltpu.VMEM, pltpu.SemaphoreType.DMA
    slab, dense = (PIECES, BLOCKS, ROWS, PIECE), (PIECES, BLOCKS * PAD_K, PIECE)
    drive, repel = pl.pallas_call(
        kernel,
        out_shape=[pltpu.VMEM((ROWS, COLS), f32)] * 2,
        in_specs=[pl.BlockSpec(memory_space=pl.ANY)] * 2 + [pl.BlockSpec(memory_space=pltpu.SMEM)],
        out_specs=[pl.BlockSpec(memory_space=pltpu.VMEM)] * 2,
        scratch_shapes=[
            vmem(slab, bf16), vmem(slab, bf16), vmem(dense, bf16), vmem(dense, bf16),
            vmem((len(SUPER), 2 * PAD_K, 2 * PAD_K), f32), vmem((FLAT, 128), f32), vmem((FLAT, 128), bf16),
            vmem((PARTS, HALF, 128), bf16), vmem((PARTS, HALF, 128), f32), vmem((PARTS, HALF, 128), bf16),
            vmem((PARTS, 4, QUARTER, 128), bf16), vmem((PARTS, QUARTER, 128), f32), vmem((PARTS, 16, CHUNK, 128), f32),
            vmem((FLAT, 128), bf16), vmem((FLAT, 128), f32), vmem((BLOCKS * PAD_M, BLOCKS * PAD_K), bf16),
            vmem((BLOCKS, ROWS, 1), f32), vmem((BLOCKS * PAD_M, PIECE), f32),
            vmem(slab, bf16), vmem(slab, bf16), vmem(slab, bf16), vmem(slab, bf16),
        ]
        + [dma((PIECES, BLOCKS))] * 2 + [dma((G_PIECES, BLOCKS))] * 2 + [dma((PIECES, BLOCKS))] * 4 + [dma((2, PIECES))]
        + [dma((PARTS,))] * 2 + [dma((PARTS, 4))] * 2
        + [dma((PARTS, 16))] * 4 + [dma((PARTS, 4))] * 4,
        compiler_params=pltpu.CompilerParams(
            collective_id=0, has_side_effects=True, vmem_limit_bytes=44 * 2**20),
        name="svgd",
    )(particles, gradients, spread)
    return drive, repel


def solution(mesh):
    return jax.shard_map(
        per_device,
        mesh=mesh,
        in_specs=(P("dom", "feat"), P("dom", "feat"), P()),
        out_specs=(P("dom", "feat"), P("dom", "feat")),
        check_vma=False,
    )
```

time: 1380 us -> 141 us (0.10)
  blocking collectives: 849 us -> 0 us
  waiting for transfers between devices: 357 us -> 0 us
  Pallas kernels: 0 us -> 135 us
  matrix products: 68.5 us -> 0 us
  local copies, waits for them, and re-layouts: 66.5 us -> 4.63 us
  starting transfers between devices: 16.7 us -> 0 us
    psum x8 -> x0, blocking collectives: 849 us -> none  [add_tile(): dist = lax.psum(partial_value, 'feat')]
    ppermute x14 -> x0, waiting for transfers between devices: 357 us -> none  [passed_along(): return lax.ppermute(value, axis, pairs)]
    pallas_call x0 -> x1, Pallas kernels: none -> 135 us  [per_device(): pl.pallas_call(kernel, out_shape=[pltpu.VMEM((ROWS, COLS), f32)] * 2, in_...]
    dot_general x24 -> x0, matrix products: 68.5 us -> none  [the longest x8 29.9 us: add_tile(): jnp.dot(kern, other_g, preferred_element_type=jnp.float32)]
    while x98 -> x0, local copies, waits for them, and re-layouts: 59.7 us -> none
    ppermute x14 -> x0, starting transfers between devices: 16.7 us -> none  [passed_along(): return lax.ppermute(value, axis, pairs)]
  transfers between devices with their start and end apart: 14 -> 0, of which waited for: 7 -> 0; matrix products, arithmetic and copies ran while one was open for 2% -> 0% of each run, Pallas kernels for 0% -> 0%
where the time goes in v2:
time: 141 us
  Pallas kernels  135 us (96%)
  local copies, waits for them, and re-layouts  4.63 us (3%)
    pallas_call x1, Pallas kernels, per_device(): pl.pallas_call(kernel, out_shape=[pltpu.VMEM((ROWS, COLS), f32)] * 2, in_...  135 us
    unnamed x2, local copies, waits for them, and re-layouts  4.63 us

profile of v2, /device:TPU:1, one launch (start us, length us, event | category | flops | bytes accessed | tf_op | source)
XLA Modules:
  0.0 141.3 jit_solution(8500103991015052750)
XLA Ops:
  1.3 135.4 %svgd.1 = (f32[104,12288]{1,0:T(8,128)S(1)}, f32[104,12288]{1,0:T(8,128)S(1)}) custom-call(bf16[104,12288]{1,0:T(8,128)(2,1)} %x.1, bf16[104,12288]{1,0:T(8,128)(2,1)} %g.1, f32[1]{0:T(128)S(6)} %copy.9.spread), custom_call_target="tpu_custom_call" | custom-call | tf_op jit(solution)/shard_map/svgd/pallas_call | solution.py:347
  136.7 2.3 %copy.7 = f32[104,12288]{1,0:T(8,128)} copy(f32[104,12288]{1,0:T(8,128)S(1)} %get-tuple-element.2) | data formatting | bytes 10223616
  139.0 2.3 %copy.8 = f32[104,12288]{1,0:T(8,128)} copy(f32[104,12288]{1,0:T(8,128)S(1)} %get-tuple-element.3) | data formatting | bytes 10223616

commit v3 on v2

--- a/solution.py
+++ b/solution.py
@@ -13,9 +13,10 @@
 PIECES = 3
 WIDTH = COLS // BLOCKS
 PIECE = WIDTH // PIECES
-G_PIECES = 6
+G_PIECES = 12
 G_PIECE = WIDTH // G_PIECES
-G_AT = (1, 0, 1, 1, 1, 2)
+G_RATIO = G_PIECES // PIECES
+G_AT = (2, 2, 1, 0, 1, 1, 5)
 PARTS = 2
 FLAT = 4096
 PART = FLAT // PARTS
@@ -28,6 +29,9 @@
             if 2 * si + a <= 2 * sj + b:
                 PAIRS.append((2 * si + a, 2 * sj + b, n, a * PAD_K, b * PAD_K))
 FIRST = [n for n in range(len(PAIRS)) if (n + 1) * ROWS <= PART]
+HOPS = (0, 1, 2, 1)
+PLANE = sorted(range(1, 16), key=lambda r: -HOPS[r // 4] - HOPS[r % 4])
+RING = (2, 1, 3)
 MESH = pl.DeviceIdType.MESH
 
 
@@ -78,6 +82,9 @@
         return pltpu.make_async_remote_copy(
             src_ref=src, dst_ref=dst, send_sem=send, recv_sem=recv, device_id=device, device_id_type=MESH)
 
+    def all_of(ref, sem):
+        pltpu.make_async_copy(ref, ref, sem).wait()
+
     def inward(src, dst, send, recv, c, r):
         to = dom_peer(r)
         return remote(src.at[:, columns(to, c)], dst.at[c, dom], send.at[c, r], recv.at[c, r], (to, feat))
@@ -86,9 +93,9 @@
         return inward(x, xt, x_send, x_recv, c, r)
 
     def g_in(p, r):
-        to, lane = dom_peer(r), p % 2 * G_PIECE
+        to, lane = dom_peer(r), p % G_RATIO * G_PIECE
         source = g.at[:, pl.ds(pl.multiple_of(to * WIDTH + p * G_PIECE, 128), G_PIECE)]
-        target = gt.at[p // 2, dom, :, pl.ds(lane, G_PIECE)]
+        target = gt.at[p // G_RATIO, dom, :, pl.ds(lane, G_PIECE)]
         return remote(source, target, g_send.at[p, r], g_recv.at[p, r], (to, feat))
 
     def start_g(point):
@@ -109,15 +116,14 @@
         own_copy(x, xt, 0, c).start()
     for c in range(PIECES):
         own_copy(g, gt, 1, c).start()
-    part[...] = jnp.zeros_like(part)
-    acc[...] = jnp.zeros_like(acc)
-    xd[...] = jnp.zeros_like(xd)
-    gd[...] = jnp.zeros_like(gd)
-    full[...] = jnp.zeros_like(full)
+    part[FLAT - 3 * PAD_K :] = jnp.zeros((3 * PAD_K, 128), f32)
 
     def spread_out(src, dst, c):
-        for b in range(BLOCKS):
-            dst[c, b * PAD_K : b * PAD_K + ROWS] = src[c, b]
+        @pl.loop(0, BLOCKS)
+        def _(b):
+            start = pl.multiple_of(b * PAD_K, PAD_K)
+            dst[c, pl.ds(start + PAD_K - 32, 32)] = jnp.zeros((32, PIECE), bf16)
+            dst[c, pl.ds(start, ROWS)] = src[c, b]
 
     for c in range(PIECES):
         @pl.loop(1, BLOCKS)
@@ -138,7 +144,8 @@
         for n, (si, sj) in enumerate(SUPER):
             left = xd[c, si * 2 * PAD_K : (si + 1) * 2 * PAD_K]
             right = xd[c, sj * 2 * PAD_K : (sj + 1) * 2 * PAD_K]
-            acc[n] += lax.dot_general(left, right, (((1,), (1,)), ((), ())), preferred_element_type=f32)
+            inner = lax.dot_general(left, right, (((1,), (1,)), ((), ())), preferred_element_type=f32)
+            acc[n] = inner if c == 0 else acc[n] + inner
 
     size = (2 * PAD_K, 2 * PAD_K)
     on_diagonal = lax.broadcasted_iota(jnp.int32, size, 0) == lax.broadcasted_iota(jnp.int32, size, 1)
@@ -172,14 +179,14 @@
     def to_plane(h, r):
         m2, device = plane_peer(r)
         rows = pl.ds(pl.multiple_of(m2 * CHUNK, 8), CHUNK)
-        return remote(y_sum.at[h, rows], from_zx.at[h, r], p_send.at[h, r], p_recv.at[h, r], device)
+        return remote(y_sum.at[h, rows], from_zx.at[h, r], p_send.at[h], p_recv.at[h], device)
 
     def mine(h):
         return pl.ds(pl.multiple_of(h * PART + core * HALF + y * QUARTER + member * CHUNK, 16), CHUNK)
 
     def kern_to_plane(h, r):
         rows = kern.at[mine(h)]
-        return remote(rows, rows, ap_send.at[h, r], ap_recv.at[h, r], plane_peer(r)[1])
+        return remote(rows, rows, ap_send.at[h], ap_recv.at[h], plane_peer(r)[1])
 
     def kern_to_y(h, r):
         rows = kern.at[pl.ds(pl.multiple_of(h * PART + core * HALF + y * QUARTER, 16), QUARTER)]
@@ -195,7 +202,7 @@
         rows = pl.ds(pl.multiple_of(h * PART + core * HALF, 16), HALF)
         core_sum[h] = part[rows] + from_core[h].astype(f32)
         core_wire[h] = core_sum[h].astype(bf16)
-        for r in range(1, 4):
+        for r in RING:
             to_y(h, r).start()
     for h in range(PARTS):
         for r in range(1, 4):
@@ -205,36 +212,30 @@
             total = total + from_y[h, r].astype(f32)
         y_sum[h] = total
 
-        @pl.loop(1, 16)
-        def _(r):
+        for r in PLANE:
             to_plane(h, r).start()
 
-    start_g(3)
+        start_g(3 + h)
+
     width = DIMS * spread[0]
     for h in range(PARTS):
         from_zx[h, 0] = y_sum[h, pl.ds(pl.multiple_of(member * CHUNK, 8), CHUNK)]
 
-        @pl.loop(1, 16)
-        def _(r):
-            to_plane(h, r).wait_recv()
+        all_of(from_zx.at[h, pl.ds(1, 15)], p_recv.at[h])
 
         kern[mine(h)] = jnp.exp(-jnp.sum(from_zx[h], axis=0) / width).astype(bf16)
 
-        @pl.loop(1, 16)
-        def _(r):
+        for r in PLANE:
             kern_to_plane(h, r).start()
 
-    start_g(4)
-
-    for h in range(PARTS):
-        @pl.loop(1, 16)
-        def _(r):
-            kern_to_plane(h, r).wait_recv()
-
-        for r in range(1, 4):
+        start_g(5 + h)
+
+    for h in range(PARTS):
+        all_of(kern.at[pl.ds(0, 15 * CHUNK)], ap_recv.at[h])
+
+        for r in RING:
             kern_to_y(h, r).start()
         kern_to_core(h, 0).start()
-    start_g(5)
     for h in range(PARTS):
         for r in range(1, 4):
             kern_to_y(h, r).wait_recv()
@@ -255,13 +256,8 @@
                     across = jnp.where(real, block.T, 0.0)
                     full[b * PAD_M : b * PAD_M + ROWS, a * PAD_K : (a + 1) * PAD_K] = across[:ROWS].astype(bf16)
 
-    @pl.loop(0, BLOCKS)
-    def _(i):
-        rows = pl.ds(pl.multiple_of(i * PAD_M, 16), ROWS)
-        sums = jnp.zeros((ROWS, PAD_K), f32)
-        for k in range(BLOCKS):
-            sums = sums + full[rows, k * PAD_K : (k + 1) * PAD_K].astype(f32)
-        totals[i] = jnp.sum(sums, axis=1, keepdims=True)
+    ones = jnp.ones((BLOCKS * PAD_K, PAD_K), bf16)
+    totals[...] = jnp.dot(full[...], ones, preferred_element_type=f32)
 
     def outward(src, dst, send, recv, c, r):
         to = dom_peer(r)
@@ -278,7 +274,8 @@
 
     def repel_rows(c, i):
         here = xd[c, pl.ds(pl.multiple_of(i * PAD_K, 16), ROWS)].astype(f32)
-        return totals[i] * here - product_rows(i)
+        total = totals[pl.ds(pl.multiple_of(i * PAD_M, 8), ROWS)]
+        return jnp.concatenate([total] * (PIECE // PAD_K), axis=1) * here - product_rows(i)
 
     @pl.loop(0, PIECES)
     def _(c):
@@ -295,7 +292,7 @@
     for c in range(PIECES):
         own_copy(g, gt, 1, c).wait()
 
-        for p in (2 * c, 2 * c + 1):
+        for p in range(G_RATIO * c, G_RATIO * (c + 1)):
             @pl.loop(1, BLOCKS)
             def _(r):
                 g_in(p, r).wait()
@@ -322,10 +319,8 @@
         for r in range(4):
             kern_to_core(h, r).wait_send()
 
-        @pl.loop(1, 16)
-        def _(r):
-            to_plane(h, r).wait_send()
-            kern_to_plane(h, r).wait_send()
+        all_of(from_zx.at[h, pl.ds(1, 15)], p_send.at[h])
+        all_of(kern.at[pl.ds(0, 15 * CHUNK)], ap_send.at[h])
 
     def widen(copy, land, out):
         @pl.loop(0, PIECES)
@@ -355,12 +350,12 @@
             vmem((PARTS, HALF, 128), bf16), vmem((PARTS, HALF, 128), f32), vmem((PARTS, HALF, 128), bf16),
             vmem((PARTS, 4, QUARTER, 128), bf16), vmem((PARTS, QUARTER, 128), f32), vmem((PARTS, 16, CHUNK, 128), f32),
             vmem((FLAT, 128), bf16), vmem((FLAT, 128), f32), vmem((BLOCKS * PAD_M, BLOCKS * PAD_K), bf16),
-            vmem((BLOCKS, ROWS, 1), f32), vmem((BLOCKS * PAD_M, PIECE), f32),
+            vmem((BLOCKS * PAD_M, PAD_K), f32), vmem((BLOCKS * PAD_M, PIECE), f32),
             vmem(slab, bf16), vmem(slab, bf16), vmem(slab, bf16), vmem(slab, bf16),
         ]
         + [dma((PIECES, BLOCKS))] * 2 + [dma((G_PIECES, BLOCKS))] * 2 + [dma((PIECES, BLOCKS))] * 4 + [dma((2, PIECES))]
         + [dma((PARTS,))] * 2 + [dma((PARTS, 4))] * 2
-        + [dma((PARTS, 16))] * 4 + [dma((PARTS, 4))] * 4,
+        + [dma((PARTS,))] * 4 + [dma((PARTS, 4))] * 4,
         compiler_params=pltpu.CompilerParams(
             collective_id=0, has_side_effects=True, vmem_limit_bytes=44 * 2**20),
         name="svgd",

time: 141 us -> 139 us (0.986)
  Pallas kernels: 135 us -> 133 us
    pallas_call x1, Pallas kernels: 135 us -> 133 us  [per_device(): pl.pallas_call(kernel, out_shape=[pltpu.VMEM((ROWS, COLS), f32)] * 2, in_...]
where the time goes in v3:
time: 139 us
  Pallas kernels  133 us (96%)
  local copies, waits for them, and re-layouts  4.63 us (3%)
    pallas_call x1, Pallas kernels, per_device(): pl.pallas_call(kernel, out_shape=[pltpu.VMEM((ROWS, COLS), f32)] * 2, in_...  133 us
    unnamed x2, local copies, waits for them, and re-layouts  4.63 us

profile of v3, /device:TPU:1, one launch (start us, length us, event | category | flops | bytes accessed | tf_op | source)
XLA Modules:
  0.0 138.7 jit_solution(11120803584021440855)
XLA Ops:
  1.3 132.8 %svgd.1 = (f32[104,12288]{1,0:T(8,128)S(1)}, f32[104,12288]{1,0:T(8,128)S(1)}) custom-call(bf16[104,12288]{1,0:T(8,128)(2,1)} %x.1, bf16[104,12288]{1,0:T(8,128)(2,1)} %g.1, f32[1]{0:T(128)S(6)} %copy.9.spread), custom_call_target="tpu_custom_call" | custom-call | tf_op jit(solution)/shard_map/svgd/pallas_call | solution.py:342
  134.1 2.3 %copy.7 = f32[104,12288]{1,0:T(8,128)} copy(f32[104,12288]{1,0:T(8,128)S(1)} %get-tuple-element.2) | data formatting | bytes 10223616
  136.4 2.3 %copy.8 = f32[104,12288]{1,0:T(8,128)} copy(f32[104,12288]{1,0:T(8,128)S(1)} %get-tuple-element.3) | data formatting | bytes 10223616

commit v4 on v3

--- a/solution.py
+++ b/solution.py
@@ -13,10 +13,9 @@
 PIECES = 3
 WIDTH = COLS // BLOCKS
 PIECE = WIDTH // PIECES
-G_PIECES = 12
-G_PIECE = WIDTH // G_PIECES
-G_RATIO = G_PIECES // PIECES
-G_AT = (2, 2, 1, 0, 1, 1, 5)
+G_WIDTHS = (256, 256, 128, 128, 128, 128, 512)
+G_STARTS = tuple(sum(G_WIDTHS[:p]) for p in range(len(G_WIDTHS)))
+G_AT = (1, 1, 1, 0, 1, 1, 2)
 PARTS = 2
 FLAT = 4096
 PART = FLAT // PARTS
@@ -85,33 +84,32 @@
     def all_of(ref, sem):
         pltpu.make_async_copy(ref, ref, sem).wait()
 
-    def inward(src, dst, send, recv, c, r):
-        to = dom_peer(r)
-        return remote(src.at[:, columns(to, c)], dst.at[c, dom], send.at[c, r], recv.at[c, r], (to, feat))
-
-    def x_in(c, r):
-        return inward(x, xt, x_send, x_recv, c, r)
-
-    def g_in(p, r):
-        to, lane = dom_peer(r), p % G_RATIO * G_PIECE
-        source = g.at[:, pl.ds(pl.multiple_of(to * WIDTH + p * G_PIECE, 128), G_PIECE)]
-        target = gt.at[p // G_RATIO, dom, :, pl.ds(lane, G_PIECE)]
-        return remote(source, target, g_send.at[p, r], g_recv.at[p, r], (to, feat))
+    def inward(src, dst, send, recv, start, width, r):
+        to, c = dom_peer(r), start // PIECE
+        source = src.at[:, pl.ds(pl.multiple_of(to * WIDTH + start, 128), width)]
+        target = dst.at[c, dom, :, pl.ds(start % PIECE, width)]
+        return remote(source, target, send.at[c], recv.at[c], (to, feat))
+
+    def to_all(start_one):
+        @pl.loop(0, BLOCKS - 1)
+        def _(q):
+            start_one(BLOCKS - 1 - q)
+
+    def all_seven(slab, sem, c):
+        all_of(slab.at[c, pl.ds(0, BLOCKS - 1)], sem.at[c])
+
+    def start_x(c):
+        to_all(lambda r: inward(x, xt, x_send, x_recv, c * PIECE, PIECE, r).start())
 
     def start_g(point):
         for p in range(sum(G_AT[:point]), sum(G_AT[: point + 1])):
-            @pl.loop(1, BLOCKS)
-            def _(r):
-                g_in(p, r).start()
+            to_all(lambda r: inward(g, gt, g_send, g_recv, G_STARTS[p], G_WIDTHS[p], r).start())
 
     def own_copy(src, dst, which, c):
         return pltpu.make_async_copy(src.at[:, columns(dom, c)], dst.at[c, dom], own_sem.at[which, c])
 
-    for c in range(2):
-        @pl.loop(1, BLOCKS)
-        def _(r):
-            x_in(c, r).start()
-
+    for c in range(PIECES):
+        start_x(c)
     for c in range(PIECES):
         own_copy(x, xt, 0, c).start()
     for c in range(PIECES):
@@ -126,20 +124,11 @@
             dst[c, pl.ds(start, ROWS)] = src[c, b]
 
     for c in range(PIECES):
-        @pl.loop(1, BLOCKS)
-        def _(r):
-            x_in(c, r).wait_send()
-            if c == 0:
-                x_in(2, r).start()
-
+        all_seven(xt, x_send, c)
         if c > 0:
             start_g(c - 1)
         own_copy(x, xt, 0, c).wait()
-
-        @pl.loop(1, BLOCKS)
-        def _(r):
-            x_in(c, r).wait_recv()
-
+        all_seven(xt, x_recv, c)
         spread_out(xt, xd, c)
         for n, (si, sj) in enumerate(SUPER):
             left = xd[c, si * 2 * PAD_K : (si + 1) * 2 * PAD_K]
@@ -174,7 +163,7 @@
     def to_y(h, r):
         y2, device = y_peer(r)
         rows = pl.ds(pl.multiple_of(y2 * QUARTER, 16), QUARTER)
-        return remote(core_wire.at[h, rows], from_y.at[h, r], y_send.at[h, r], y_recv.at[h, r], device)
+        return remote(core_wire.at[h, rows], from_y.at[h, r], y_send.at[h], y_recv.at[h], device)
 
     def to_plane(h, r):
         m2, device = plane_peer(r)
@@ -205,8 +194,7 @@
         for r in RING:
             to_y(h, r).start()
     for h in range(PARTS):
-        for r in range(1, 4):
-            to_y(h, r).wait_recv()
+        all_of(from_y.at[h, pl.ds(1, 3)], y_recv.at[h])
         total = core_sum[h, pl.ds(pl.multiple_of(y * QUARTER, 16), QUARTER)]
         for r in range(1, 4):
             total = total + from_y[h, r].astype(f32)
@@ -261,7 +249,7 @@
 
     def outward(src, dst, send, recv, c, r):
         to = dom_peer(r)
-        return remote(src.at[c, to], dst.at[c, dom], send.at[c, r], recv.at[c, r], (to, feat))
+        return remote(src.at[c, to], dst.at[c, dom], send.at[c], recv.at[c], (to, feat))
 
     def r_out(c, r):
         return outward(repel_stage, repel_land, r_send, r_recv, c, r)
@@ -281,40 +269,38 @@
     def _(c):
         product[...] = jnp.dot(full[...], xd[c], preferred_element_type=f32)
 
-        @pl.loop(1, BLOCKS)
-        def _(r):
+        def one(r):
             i = dom_peer(r)
             repel_stage[c, i] = repel_rows(c, i).astype(bf16)
             r_out(c, r).start()
 
+        to_all(one)
+
         repel_out[:, columns(dom, c)] = repel_rows(c, dom)
 
     for c in range(PIECES):
         own_copy(g, gt, 1, c).wait()
 
-        for p in range(G_RATIO * c, G_RATIO * (c + 1)):
-            @pl.loop(1, BLOCKS)
-            def _(r):
-                g_in(p, r).wait()
-
+        all_seven(gt, g_recv, c)
         spread_out(gt, gd, c)
 
     @pl.loop(0, PIECES)
     def _(c):
         product[...] = jnp.dot(full[...], gd[c], preferred_element_type=f32)
 
-        @pl.loop(1, BLOCKS)
-        def _(r):
+        def one(r):
             i = dom_peer(r)
             drive_stage[c, i] = product_rows(i).astype(bf16)
             d_out(c, r).start()
 
+        to_all(one)
+
         drive_out[:, columns(dom, c)] = product_rows(dom)
 
     for h in range(PARTS):
         to_core(h).wait_send()
+        all_of(from_y.at[h, pl.ds(1, 3)], y_send.at[h])
         for r in range(1, 4):
-            to_y(h, r).wait_send()
             kern_to_y(h, r).wait_send()
         for r in range(4):
             kern_to_core(h, r).wait_send()
@@ -322,17 +308,22 @@
         all_of(from_zx.at[h, pl.ds(1, 15)], p_send.at[h])
         all_of(kern.at[pl.ds(0, 15 * CHUNK)], ap_send.at[h])
 
-    def widen(copy, land, out):
+    for c in range(PIECES):
+        all_seven(gt, g_send, c)
+
+    def widen(land, out, send, recv):
         @pl.loop(0, PIECES)
         def _(c):
+            all_seven(land, send, c)
+            all_seven(land, recv, c)
+
             @pl.loop(1, BLOCKS)
-            def _(r):
-                copy(c, r).wait()
-                source = (z + 4 - r // 2) % 4 * 2 + (x_lo + r % 2) % 2
+            def _(k):
+                source = (dom + k) % BLOCKS
                 out[:, columns(source, c)] = land[c, source].astype(f32)
 
-    widen(r_out, repel_land, repel_out)
-    widen(d_out, drive_land, drive_out)
+    widen(repel_land, repel_out, r_send, r_recv)
+    widen(drive_land, drive_out, d_send, d_recv)
 
 
 def per_device(particles, gradients, spread):
@@ -353,8 +344,8 @@
             vmem((BLOCKS * PAD_M, PAD_K), f32), vmem((BLOCKS * PAD_M, PIECE), f32),
             vmem(slab, bf16), vmem(slab, bf16), vmem(slab, bf16), vmem(slab, bf16),
         ]
-        + [dma((PIECES, BLOCKS))] * 2 + [dma((G_PIECES, BLOCKS))] * 2 + [dma((PIECES, BLOCKS))] * 4 + [dma((2, PIECES))]
-        + [dma((PARTS,))] * 2 + [dma((PARTS, 4))] * 2
+        + [dma((PIECES,))] * 8 + [dma((2, PIECES))]
+        + [dma((PARTS,))] * 4
         + [dma((PARTS,))] * 4 + [dma((PARTS, 4))] * 4,
         compiler_params=pltpu.CompilerParams(
             collective_id=0, has_side_effects=True, vmem_limit_bytes=44 * 2**20),

time: 139 us -> 134 us (0.964)
  Pallas kernels: 133 us -> 128 us
    pallas_call x1, Pallas kernels: 133 us -> 128 us  [per_device(): pl.pallas_call(kernel, out_shape=[pltpu.VMEM((ROWS, COLS), f32)] * 2, in_...]
where the time goes in v4:
time: 134 us
  Pallas kernels  128 us (96%)
  local copies, waits for them, and re-layouts  4.63 us (3%)
    pallas_call x1, Pallas kernels, per_device(): pl.pallas_call(kernel, out_shape=[pltpu.VMEM((ROWS, COLS), f32)] * 2, in_...  128 us
    unnamed x2, local copies, waits for them, and re-layouts  4.63 us

profile of v4, /device:TPU:1, one launch (start us, length us, event | category | flops | bytes accessed | tf_op | source)
XLA Modules:
  0.0 133.5 jit_solution(1772509853164664630)
XLA Ops:
  1.3 127.6 %svgd.1 = (f32[104,12288]{1,0:T(8,128)S(1)}, f32[104,12288]{1,0:T(8,128)S(1)}) custom-call(bf16[104,12288]{1,0:T(8,128)(2,1)} %x.1, bf16[104,12288]{1,0:T(8,128)(2,1)} %g.1, f32[1]{0:T(128)S(6)} %copy.9.spread), custom_call_target="tpu_custom_call" | custom-call | tf_op jit(solution)/shard_map/svgd/pallas_call | solution.py:333
  128.9 2.3 %copy.7 = f32[104,12288]{1,0:T(8,128)} copy(f32[104,12288]{1,0:T(8,128)S(1)} %get-tuple-element.2) | data formatting | bytes 10223616
  131.2 2.3 %copy.8 = f32[104,12288]{1,0:T(8,128)} copy(f32[104,12288]{1,0:T(8,128)S(1)} %get-tuple-element.3) | data formatting | bytes 10223616

commit v5 on v4

--- a/solution.py
+++ b/solution.py
@@ -10,12 +10,12 @@
 PAD_K, PAD_M = 128, 112
 COLS = 12288
 BLOCKS = 8
-PIECES = 3
+PIECES = 2
 WIDTH = COLS // BLOCKS
 PIECE = WIDTH // PIECES
 G_WIDTHS = (256, 256, 128, 128, 128, 128, 512)
 G_STARTS = tuple(sum(G_WIDTHS[:p]) for p in range(len(G_WIDTHS)))
-G_AT = (1, 1, 1, 0, 1, 1, 2)
+G_AT = (2, 0, 1, 0, 1, 1, 2)
 PARTS = 2
 FLAT = 4096
 PART = FLAT // PARTS
@@ -63,8 +63,7 @@
 
     barrier = pltpu.get_barrier_semaphore()
 
-    @pl.loop(1, 16)
-    def _(r):
+    for r in PLANE:
         pl.semaphore_signal(barrier, inc=1, device_id=plane_peer(r)[1], device_id_type=MESH)
 
     @pl.loop(1, 4)
@@ -221,9 +220,9 @@
     for h in range(PARTS):
         all_of(kern.at[pl.ds(0, 15 * CHUNK)], ap_recv.at[h])
 
+        kern_to_core(h, 0).start()
         for r in RING:
             kern_to_y(h, r).start()
-        kern_to_core(h, 0).start()
     for h in range(PARTS):
         for r in range(1, 4):
             kern_to_y(h, r).wait_recv()

time: 134 us -> 133 us (level)
  no operation moved by 1% of the time
where the time goes in v5:
time: 133 us
  Pallas kernels  127 us (95%)
  local copies, waits for them, and re-layouts  4.63 us (3%)
    pallas_call x1, Pallas kernels, per_device(): pl.pallas_call(kernel, out_shape=[pltpu.VMEM((ROWS, COLS), f32)] * 2, in_...  127 us
    unnamed x2, local copies, waits for them, and re-layouts  4.63 us

profile of v5, /device:TPU:1, one launch (start us, length us, event | category | flops | bytes accessed | tf_op | source)
XLA Modules:
  0.0 132.6 jit_solution(877101793100610315)
XLA Ops:
  1.3 126.7 %svgd.1 = (f32[104,12288]{1,0:T(8,128)S(1)}, f32[104,12288]{1,0:T(8,128)S(1)}) custom-call(bf16[104,12288]{1,0:T(8,128)(2,1)} %x.1, bf16[104,12288]{1,0:T(8,128)(2,1)} %g.1, f32[1]{0:T(128)S(6)} %copy.9.spread), custom_call_target="tpu_custom_call" | custom-call | tf_op jit(solution)/shard_map/svgd/pallas_call | solution.py:332
  128.0 2.3 %copy.7 = f32[104,12288]{1,0:T(8,128)} copy(f32[104,12288]{1,0:T(8,128)S(1)} %get-tuple-element.2) | data formatting | bytes 10223616
  130.3 2.3 %copy.8 = f32[104,12288]{1,0:T(8,128)} copy(f32[104,12288]{1,0:T(8,128)S(1)} %get-tuple-element.3) | data formatting | bytes 10223616

commit v6 on v5

--- a/solution.py
+++ b/solution.py
@@ -123,7 +123,7 @@
             dst[c, pl.ds(start, ROWS)] = src[c, b]
 
     for c in range(PIECES):
-        all_seven(xt, x_send, c)
+        all_of(x.at[:, pl.ds(0, (BLOCKS - 1) * PIECE)], x_send.at[c])
         if c > 0:
             start_g(c - 1)
         own_copy(x, xt, 0, c).wait()
@@ -308,7 +308,7 @@
         all_of(kern.at[pl.ds(0, 15 * CHUNK)], ap_send.at[h])
 
     for c in range(PIECES):
-        all_seven(gt, g_send, c)
+        all_of(g.at[:, pl.ds(0, (BLOCKS - 1) * PIECE)], g_send.at[c])
 
     def widen(land, out, send, recv):
         @pl.loop(0, PIECES)

time: 133 us -> 133 us (level)
  no operation moved by 1% of the time
where the time goes in v6:
time: 133 us
  Pallas kernels  127 us (95%)
  local copies, waits for them, and re-layouts  4.63 us (3%)
    pallas_call x1, Pallas kernels, per_device(): pl.pallas_call(kernel, out_shape=[pltpu.VMEM((ROWS, COLS), f32)] * 2, in_...  127 us
    unnamed x2, local copies, waits for them, and re-layouts  4.63 us

profile of v6, /device:TPU:1, one launch (start us, length us, event | category | flops | bytes accessed | tf_op | source)
XLA Modules:
  0.0 132.6 jit_solution(877101793100610315)
XLA Ops:
  1.3 126.7 %svgd.1 = (f32[104,12288]{1,0:T(8,128)S(1)}, f32[104,12288]{1,0:T(8,128)S(1)}) custom-call(bf16[104,12288]{1,0:T(8,128)(2,1)} %x.1, bf16[104,12288]{1,0:T(8,128)(2,1)} %g.1, f32[1]{0:T(128)S(6)} %copy.9.spread), custom_call_target="tpu_custom_call" | custom-call | tf_op jit(solution)/shard_map/svgd/pallas_call | solution.py:332
  128.0 2.3 %copy.7 = f32[104,12288]{1,0:T(8,128)} copy(f32[104,12288]{1,0:T(8,128)S(1)} %get-tuple-element.2) | data formatting | bytes 10223616
  130.3 2.3 %copy.8 = f32[104,12288]{1,0:T(8,128)} copy(f32[104,12288]{1,0:T(8,128)S(1)} %get-tuple-element.3) | data formatting | bytes 10223616
